TPU v7x, 512 devices: a whole 4x4x16 slice. The times are simulated.
512 devices in a mesh: lab: 32 (over z_lo, y, core), img: 16 (over x, z_hi).
Axes of the slice: x: 4, y: 4, z: 16 (z_hi: 4, z_lo: 4; z = z_hi * 4 + z_lo), core: 2. Of those that a mesh axis runs over, the one named last changes fastest.
Arguments:
- queries: bfloat16 [32768, 512], P('lab'), may hold values from -12 to 12
- keys: bfloat16 [16, 576, 512], P('img', 'lab'), may hold values from -5 to 5
- values: bfloat16 [16, 576, 512], P('img', 'lab'), may hold values from -6 to 6
- grad_out: bfloat16 [16, 32768, 512], P('img', 'lab'), may hold values from -6 to 6
- block_mask: int32 [256, 16], P('lab', 'img'), may hold values from 0 to 1, as said below
Outputs:
- grad_queries: bfloat16 [32768, 512], P(('lab', 'img'))
- grad_keys: bfloat16 [16, 576, 512], P('img', 'lab')
- grad_values: bfloat16 [16, 576, 512], P('img', 'lab')
Inputs may be any that keep to these rules, and one draw needn't show every extreme that they name: `block_mask`: each label block has its own density of images that it reads.
All inputs are finite; a program needn't handle non-finite values.
Results may differ from a plain program's by a relative error of at most 0.0061.
Values may be sent and summed in bfloat16 or wider, within the bound.
A program may use at most 128 MiB of HBM per device.

v0:
```python
import math
import jax
import jax.numpy as jnp
from jax import lax
from jax.sharding import PartitionSpec as P

H = 8
E = 64


def attend(query_block, grad_block, key_image, value_image, weight):
    scale = 1.0 / math.sqrt(E)
    scores = (
        jnp.einsum("lhe,phe->lhp", query_block, key_image, preferred_element_type=jnp.float32)
        * scale
    )
    probs = jax.nn.softmax(scores, axis=-1)
    dprobs = jnp.einsum("lhe,phe->lhp", grad_block, value_image, preferred_element_type=jnp.float32)
    delta = jnp.sum(probs * dprobs, axis=-1, keepdims=True)
    masked = (probs * weight).astype(jnp.bfloat16)
    dscores = (weight * probs * (dprobs - delta) * scale).astype(jnp.bfloat16)
    query_grad = jnp.einsum("lhp,phe->lhe", dscores, key_image, preferred_element_type=jnp.float32)
    return (masked, dscores, query_grad)


def body(queries, keys, values, grad_out, block_mask):
    lab_rows, feature_width = queries.shape
    blocks = block_mask.shape[0]
    img_count = keys.shape[0]
    block_rows = lab_rows // blocks
    keys_full, values_full = (
        lax.all_gather(keys, "lab", axis=1, tiled=True),
        lax.all_gather(values, "lab", axis=1, tiled=True),
    )
    patches = keys_full.shape[1]
    query_blocks = queries.reshape(blocks, block_rows, H, E)
    grad_blocks = grad_out.reshape(img_count, blocks, block_rows, H, E)
    weights = block_mask.astype(jnp.float32)
    key_image = keys_full[0].reshape(patches, H, E)
    value_image = values_full[0].reshape(patches, H, E)

    def run_block(carry, pieces):
        query_block, grad_block, weight = pieces
        masked, dscores, query_grad = attend(
            query_block, grad_block, key_image, value_image, weight
        )
        dk_acc, dv_acc = carry
        dk_acc = dk_acc + jnp.einsum(
            "lhp,lhe->phe", dscores, query_block, preferred_element_type=jnp.float32
        )
        dv_acc = dv_acc + jnp.einsum(
            "lhp,lhe->phe", masked, grad_block, preferred_element_type=jnp.float32
        )
        return ((dk_acc, dv_acc), query_grad)

    zero_acc = jnp.zeros((patches, H, E), jnp.float32)
    (dk_acc, dv_acc), query_grads = lax.scan(
        run_block, (zero_acc, zero_acc), (query_blocks, grad_blocks[0], weights[:, 0])
    )
    key_terms = [dk_acc.reshape(patches, feature_width)]
    value_terms = [dv_acc.reshape(patches, feature_width)]
    key_stack = jnp.stack(key_terms)
    value_stack = jnp.stack(value_terms)
    key_sum = lax.psum_scatter(key_stack, "lab", scatter_dimension=1, tiled=True)
    value_sum = lax.psum_scatter(value_stack, "lab", scatter_dimension=1, tiled=True)
    grad_keys = key_sum.astype(jnp.bfloat16)
    grad_values = value_sum.astype(jnp.bfloat16)
    summed = lax.psum_scatter(
        query_grads.reshape(lab_rows, feature_width), "img", scatter_dimension=0, tiled=True
    )
    grad_queries = summed.astype(jnp.bfloat16)
    return (grad_queries, grad_keys, grad_values)


def solution(mesh):
    return jax.shard_map(
        body,
        mesh=mesh,
        in_specs=(
            P("lab", None),
            P("img", "lab", None),
            P("img", "lab", None),
            P("img", "lab", None),
            P("lab", "img"),
        ),
        out_specs=(P(("lab", "img"), None), P("img", "lab", None), P("img", "lab", None)),
        check_vma=False,
    )
```

profile of v0, /device:TPU:1, one launch (start us, length us, event | category | flops | bytes accessed | tf_op | source)
XLA Modules:
  0.0 575.3 jit_solution(8856966647616170280)
XLA Ops:
  7.2 2.9 reshape.17
  10.1 1.9 copy.43
  12.1 1.1 reshape.18
  13.2 1.9 copy.44
  15.1 49.2 %all_gather.6 = bf16[1,576,512]{2,0,1:T(2,128)(2,1)S(1)} all-gather(bf16[1,18,512]{2,0,1:T(2,128)(2,1)S(1)} %copy.38), channel_id=1, replica_groups=mesh['lab'=32,'img'=16] {'lab'}, dimensions={1}, use_global_device_ids=true | all-gather | bytes 608256 | tf_op jit(solution)/shard_map/all_gather | solution.py:32
  64.3 2.5 copy.39
  66.8 41.1 %all_gather.7 = bf16[1,576,512]{2,0,1:T(2,128)(2,1)S(1)} all-gather(bf16[1,18,512]{2,0,1:T(2,128)(2,1)S(1)} %copy.41), channel_id=1, replica_groups=mesh['lab'=32,'img'=16] {'lab'}, dimensions={1}, use_global_device_ids=true | all-gather | bytes 608256 | tf_op jit(solution)/shard_map/all_gather | solution.py:33
  107.9 1.6 copy.42
  109.5 162.1 %while.15 = (s32[]{:T(128)}, f32[576,8,64]{0,2,1:T(8,128)}, f32[576,8,64]{0,2,1:T(8,128)}, f32[8,128,8,64]{1,3,2,0:T(8,128)}, bf16[8,128,8,64]{1,3,2,0:T(8,128)(...) while((s32[]{:T(128)}, f32[576,8,64]{0,2,1:T(8,128)}, ...), condition=%wide.region_4.5_spmd.clone, body=%wide.region_0.4_spmd.clone.sunk | while | flops 391646912 | bytes 33648772 | solution.py:57
  109.5 3.6 fusion.79
  113.1 1.5 fusion.78
  114.5 0.6 dynamic_slice.51
  115.1 4.9 fusion.82
  120.0 4.0 fusion.81
  124.0 5.1 fusion.80
  129.1 3.6 fusion.79
  132.7 1.5 fusion.78
  134.8 4.9 fusion.82
  139.6 4.4 fusion.81
  144.0 5.5 fusion.80
  149.5 3.6 fusion.79
  153.1 1.5 fusion.78
  155.1 4.9 fusion.82
  160.0 4.4 fusion.81
  164.4 5.5 fusion.80
  169.8 3.6 fusion.79
  173.4 1.5 fusion.78
  174.9 0.6 dynamic_slice.51
  175.5 4.9 fusion.82
  180.3 4.4 fusion.81
  184.7 5.5 fusion.80
  190.2 3.6 fusion.79
  193.8 1.5 fusion.78
  195.8 4.9 fusion.82
  200.7 4.4 fusion.81
  205.1 5.5 fusion.80
  210.5 3.6 fusion.79
  214.1 1.5 fusion.78
  216.2 4.9 fusion.82
  221.0 4.4 fusion.81
  225.4 5.5 fusion.80
  230.9 3.6 fusion.79
  234.5 1.5 fusion.78
  236.5 4.8 fusion.82
  241.4 4.4 fusion.81
  245.7 5.5 fusion.80
  251.2 3.6 fusion.79
  254.8 1.5 fusion.78
  256.9 4.9 fusion.82
  261.7 4.4 fusion.81
  266.1 5.5 fusion.80
  271.6 3.9 copy.57
  275.4 4.8 reshape.19
  280.2 1.3 copy-done
  281.5 1.3 copy.46
  282.8 2.9 copy.47
  285.7 1.3 dynamic-slice
  287.6 247.9 %all-reduce.4 = (bf16[1,576,512]{2,0,1:T(2,128)(2,1)S(1)}, bf16[1,576,512]{2,0,1:T(2,128)(2,1)}) all-reduce(f32[1,576,512]{2,0,1:T(1,128)S(1)} %copy.46, f32[1,576,512]{2,0,1:T(1,128)S(1)} %copy.47), channel_id=3, replica_groups=mesh['lab'=32,'img'=16] {'lab'}, use_global_device_ids=true, to_apply=%region_6.7.clone | all-reduce | flops 589824 | bytes 3538944
  535.5 0.8 dynamic-slice_convert_fusion
  536.3 0.6 copy.49
  536.9 0.6 copy.50
  537.5 29.2 %reduce-scatter.4.cloned.1.call-done = f32[64,512]{1,0:T(8,128)} async-done(((f32[1024,512]{1,0:T(8,128)}), f32[64,512]{1,0:T(8,128)}) %reduce-scatter.4.cloned.1.call-update) | async-done | bytes 131088
  566.7 1.0 copy.56
  567.7 0.7 copy.48
  (23 shorter events, 3.7 us)
Async XLA Ops:
  7.2 559.5 %reduce-scatter.4.cloned.1.call-start = ((), (), s32[]{:S(2)}) async-start(), calls=%async_computation.1 | async-start | bytes 2228224
  7.2 4.8 copy-start.1
  12.1 3.0 copy-start.2
  13.2 53.6 %copy-start.3 = (bf16[1,18,512]{2,1,0:T(8,128)(2,1)S(1)}, bf16[1,18,512]{2,1,0:T(8,128)(2,1)}, u32[]{:S(2)}) copy-start(bf16[1,18,512]{2,1,0:T(8,128)(2,1)} %param.9) | copy-start | bytes 55300
  64.3 45.2 %copy-start.4 = (s32[8,1]{0,1:T(1,128)S(1)}, s32[8,1]{0,1:T(1,128)}, u32[]{:S(2)}) copy-start(s32[8,1]{0,1:T(1,128)} %param.11) | copy-start | bytes 100
  280.2 1.3 copy-start
Sparse Core Ops, SparseCore 0:
  280.3 286.3 reduce-scatter.3
where the time goes:
time: 576 us; the launch traced here: 575 us
  blocking collectives  338 us (59%)
  matrix products  157 us (27%)
  local copies, waits for them, and re-layouts  35.8 us (6%)
  waiting for transfers between devices  29.2 us (5%)
  between operations  14.8 us (3%)
    unnamed x1, blocking collectives  248 us
    all_gather x1, blocking collectives, body(): lax.all_gather(keys, 'lab', axis=1, tiled=True)  49.2 us
    dot_general x8, matrix products, run_block(): jnp.einsum('lhp,lhe->phe', dscores, query_block, preferred_element_type=j...  43.4 us
    all_gather x1, blocking collectives, body(): lax.all_gather(values, 'lab', axis=1, tiled=True)  41.1 us
    dot_general x8, matrix products, attend(): jnp.einsum('lhp,phe->lhe', dscores, key_image, preferred_element_type=jnp...  38.9 us
    dot_general x8, matrix products, run_block(): jnp.einsum('lhp,lhe->phe', masked, grad_block, preferred_element_type=jnp...  34.7 us
    unnamed x2, waiting for transfers between devices  29.2 us
    sub x8, matrix products, attend(): probs = jax.nn.softmax(scores, axis=-1)  28.7 us
  transfers between devices with their start and end apart: 1, of which 1 were waited for; matrix products, arithmetic and copies ran while one was open for 1% of the time, Pallas kernels for 0%

commit v1 on v0

--- a/solution.py
+++ b/solution.py
@@ -29,7 +29,9 @@
     img_count = keys.shape[0]
     block_rows = lab_rows // blocks
     keys_full, values_full = (
-        lax.all_gather(keys, "lab", axis=1, tiled=True),
+        jnp.concatenate(
+            lax.all_to_all(jnp.stack([keys] * lax.axis_size("lab")), "lab", 0, 0), axis=1
+        ),
         lax.all_gather(values, "lab", axis=1, tiled=True),
     )
     patches = keys_full.shape[1]

time: 576 us -> 549 us (0.953)
  blocking collectives: 338 us -> 295 us
  starting transfers between devices: 0.04 us -> 10.5 us
    all_gather x1 -> x0, blocking collectives: 49.2 us -> none  [body(): lax.all_gather(keys, 'lab', axis=1, tiled=True)]
    all_to_all x0 -> x1, starting transfers between devices: none -> 10.4 us  [body(): lax.all_to_all(jnp.stack([keys] * lax.axis_size('lab')), 'lab', 0, 0)]
    unnamed x21 -> x17, local copies, waits for them, and re-layouts: 18.1 us -> 18.7 us
  transfers between devices with their start and end apart: 1 -> 2, of which waited for: 1 -> 1; matrix products, arithmetic and copies ran while one was open for 1% -> 3% of each run, Pallas kernels for 0% -> 0%
where the time goes in v1:
time: 549 us; the launch traced here: 547 us
  blocking collectives  295 us (54%)
  matrix products  157 us (29%)
  local copies, waits for them, and re-layouts  37.9 us (7%)
  waiting for transfers between devices  32.1 us (6%)
  between operations  14.8 us (3%)
  starting transfers between devices  10.5 us (2%)
    unnamed x1, blocking collectives  248 us
    all_gather x1, blocking collectives, body(): lax.all_gather(values, 'lab', axis=1, tiled=True)  46.7 us
    dot_general x8, matrix products, run_block(): jnp.einsum('lhp,lhe->phe', dscores, query_block, preferred_element_type=j...  43.4 us
    dot_general x8, matrix products, attend(): jnp.einsum('lhp,phe->lhe', dscores, key_image, preferred_element_type=jnp...  38.9 us
    dot_general x8, matrix products, run_block(): jnp.einsum('lhp,lhe->phe', masked, grad_block, preferred_element_type=jnp...  34.7 us
    unnamed x2, waiting for transfers between devices  32.1 us
    sub x8, matrix products, attend(): probs = jax.nn.softmax(scores, axis=-1)  28.7 us
    unnamed x17, local copies, waits for them, and re-layouts  18.7 us
  transfers between devices with their start and end apart: 2, of which 1 were waited for; matrix products, arithmetic and copies ran while one was open for 3% of the time, Pallas kernels for 0%

profile of v1, /device:TPU:1, one launch (start us, length us, event | category | flops | bytes accessed | tf_op | source)
XLA Modules:
  0.0 547.3 jit_solution(9081872651115239589)
XLA Ops:
  7.2 1.7 stack.2
  8.9 10.4 %all-to-all-start = ((bf16[32,1,18,512]{3,2,1,0:T(8,128)(2,1)}), bf16[32,1,18,512]{3,2,1,0:T(8,128)(2,1)S(1)}, u32[]{:S(2)}, u32[]{:S(2)}) async-start(bf16[32,1,18,512]{3,2,1,0:T(8,128)(2,1)} %stack.2), calls=%async_computation | async-start | bytes 1572864 | tf_op jit(solution)/shard_map/all_to_all | solution.py:33
  19.4 2.8 reshape.20
  22.2 1.9 copy.40
  24.1 2.8 reshape.21
  26.9 1.9 copy.42
  28.9 46.7 %all_gather.3 = bf16[1,576,512]{2,0,1:T(2,128)(2,1)S(1)} all-gather(bf16[1,18,512]{2,0,1:T(2,128)(2,1)S(1)} %copy.38), channel_id=1, replica_groups=mesh['lab'=32,'img'=16] {'lab'}, dimensions={1}, use_global_device_ids=true | all-gather | bytes 608256 | tf_op jit(solution)/shard_map/all_gather | solution.py:35
  75.6 1.6 copy.39
  77.2 0.7 reshape_squeeze_reshape.3
  77.8 1.8 copy.41
  79.7 162.1 %while.15 = (s32[]{:T(128)}, f32[576,8,64]{0,2,1:T(8,128)}, f32[576,8,64]{0,2,1:T(8,128)}, f32[8,128,8,64]{1,3,2,0:T(8,128)}, bf16[8,128,8,64]{1,3,2,0:T(8,128)(...) while((s32[]{:T(128)}, f32[576,8,64]{0,2,1:T(8,128)}, ...), condition=%wide.region_4.5_spmd.clone, body=%wide.region_0.4_spmd.clone.sunk | while | flops 391646912 | bytes 33648772 | solution.py:59
  79.7 3.6 fusion.79
  83.3 1.5 fusion.78
  85.3 4.9 fusion.82
  90.2 4.0 fusion.81
  94.2 5.1 fusion.80
  99.3 3.6 fusion.79
  102.9 1.5 fusion.78
  105.0 4.9 fusion.82
  109.8 4.4 fusion.81
  114.2 5.5 fusion.80
  119.7 3.6 fusion.79
  123.3 1.5 fusion.78
  125.3 4.9 fusion.82
  130.2 4.4 fusion.81
  134.6 5.5 fusion.80
  140.0 3.6 fusion.79
  143.6 1.5 fusion.78
  145.7 4.9 fusion.82
  150.5 4.4 fusion.81
  154.9 5.5 fusion.80
  160.4 3.6 fusion.79
  164.0 1.5 fusion.78
  165.4 0.6 dynamic_slice.51
  166.0 4.9 fusion.82
  170.9 4.4 fusion.81
  175.3 5.5 fusion.80
  180.7 3.6 fusion.79
  184.3 1.5 fusion.78
  186.4 4.9 fusion.82
  191.2 4.4 fusion.81
  195.6 5.5 fusion.80
  201.1 3.6 fusion.79
  204.7 1.5 fusion.78
  206.7 4.8 fusion.82
  211.6 4.4 fusion.81
  215.9 5.5 fusion.80
  221.4 3.6 fusion.79
  225.0 1.5 fusion.78
  227.0 4.9 fusion.82
  231.9 4.4 fusion.81
  236.3 5.5 fusion.80
  241.8 3.9 copy.55
  245.6 4.8 reshape.22
  250.4 1.4 dynamic-slice
  252.4 1.3 copy.44
  253.7 2.9 copy.45
  256.6 247.9 %all-reduce.4 = (bf16[1,576,512]{2,0,1:T(2,128)(2,1)S(1)}, bf16[1,576,512]{2,0,1:T(2,128)(2,1)}) all-reduce(f32[1,576,512]{2,0,1:T(1,128)S(1)} %copy.44, f32[1,576,512]{2,0,1:T(1,128)S(1)} %copy.45), channel_id=3, replica_groups=mesh['lab'=32,'img'=16] {'lab'}, use_global_device_ids=true, to_apply=%region_6.7.clone | all-reduce | flops 589824 | bytes 3538944
  504.5 0.8 dynamic-slice_convert_fusion
  505.3 0.6 copy.47
  506.0 0.6 copy.48
  506.6 32.1 %reduce-scatter.4.cloned.1.call-done = f32[64,512]{1,0:T(8,128)} async-done(((f32[1024,512]{1,0:T(8,128)}), f32[64,512]{1,0:T(8,128)}) %reduce-scatter.4.cloned.1.call-update) | async-done | bytes 131088
  538.7 1.0 copy.54
  539.7 0.7 copy.46
  (21 shorter events, 4.2 us)
Async XLA Ops:
  8.9 68.3 %all-to-all-start = ((bf16[32,1,18,512]{3,2,1,0:T(8,128)(2,1)}), bf16[32,1,18,512]{3,2,1,0:T(8,128)(2,1)S(1)}, u32[]{:S(2)}, u32[]{:S(2)}) async-start(bf16[32,1,18,512]{3,2,1,0:T(8,128)(2,1)} %stack.2), calls=%async_computation | async-start | bytes 1572864 | tf_op jit(solution)/shard_map/all_to_all | solution.py:33
  19.3 519.4 %reduce-scatter.4.cloned.1.call-start = ((), (), s32[]{:S(2)}) async-start(), calls=%async_computation.2 | async-start | bytes 2228224
  24.1 4.7 copy-start.1
  26.9 50.3 %copy-start.2 = (s32[8,1]{0,1:T(1,128)S(1)}, s32[8,1]{0,1:T(1,128)}, u32[]{:S(2)}) copy-start(s32[8,1]{0,1:T(1,128)} %param.11) | copy-start | bytes 100
  250.4 2.1 copy-start
Sparse Core Ops, SparseCore 0:
  250.5 288.0 reduce-scatter.3
